TPU v7x, 256 devices: a whole 4x4x8 slice. The times are simulated.
256 devices in a mesh: pb: 8 (over y_hi, x), mem: 32 (over y_lo, z, core).
Axes of the slice: x: 4, y: 4 (y_hi: 2, y_lo: 2; y = y_hi * 2 + y_lo), z: 8, core: 2. Of those that a mesh axis runs over, the one named last changes fastest.
Arguments:
- queries: bfloat16 [2048, 2048], P('pb'), may hold values from -12 to 12
- keys: bfloat16 [32768, 2048], P('mem'), may hold values from -12 to 12
- values: bfloat16 [32768, 2048], P('mem'), may hold values from -6 to 6
- d_out: bfloat16 [2048, 2048], P('pb'), may hold values from -6 to 6
Outputs:
- query_grad: float32 [2048, 2048], P(('pb', 'mem'))
- key_grad: bfloat16 [32, 1024, 2048], P('mem', 'pb')
- value_grad: bfloat16 [32, 1024, 2048], P('mem', 'pb')
All inputs are finite; a program needn't handle non-finite values.
Results may differ from a plain program's by a relative error of at most 0.022.
Values may be sent and summed in bfloat16 or wider, within the bound.
A program may use at most 192 MiB of HBM per device.

v0:
```python
import jax
import jax.numpy as jnp
from jax import lax
from jax.sharding import PartitionSpec as P

H = 16
DH = 128


def scored(q3, kb):
    return jnp.einsum("rhd,jhd->hrj", q3, kb, preferred_element_type=jnp.float32) * DH ** (-0.5)


def weights(scores, row_max, row_total):
    return (jnp.exp(scores - row_max[:, :, None]) / row_total[:, :, None]).astype(jnp.bfloat16)


def grads(q3, do3, row_max, row_total, row_term, kb, vb):
    probs = weights(scored(q3, kb), row_max, row_total)
    dprobs = jnp.einsum("rhd,jhd->hrj", do3, vb, preferred_element_type=jnp.float32)
    dscores = (probs.astype(jnp.float32) * (dprobs - row_term[:, :, None])).astype(jnp.bfloat16)
    dq_part = jnp.einsum("hrj,jhd->rhd", dscores, kb, preferred_element_type=jnp.float32)
    dk_part = jnp.einsum("hrj,rhd->jhd", dscores, q3, preferred_element_type=jnp.float32)
    dv_part = jnp.einsum("hrj,rhd->jhd", probs, do3, preferred_element_type=jnp.float32)
    return (dq_part, dk_part, dv_part)


def shards(queries, keys, values, d_out):
    scale = DH ** (-0.5)
    rows = queries.shape[0]
    slots = keys.shape[0]
    q3 = queries.reshape(rows, H, DH)
    do3 = d_out.reshape(rows, H, DH)
    k3 = keys.reshape(slots, H, DH)
    v3 = values.reshape(slots, H, DH)
    blk = min(512, slots)
    nblk = slots // blk

    def piece(arr, step):
        return lax.dynamic_slice_in_dim(arr, step * blk, blk, 0)

    lowest = jnp.full((H, rows), -jnp.inf, jnp.float32)
    zeros = jnp.zeros((H, rows), jnp.float32)

    def max_step(step, acc):
        return jnp.maximum(acc, jnp.max(scored(q3, piece(k3, step)), axis=-1))

    row_max = lax.pmax(lax.fori_loop(0, nblk, max_step, lowest), "mem")

    def total_step(step, acc):
        return acc + jnp.sum(jnp.exp(scored(q3, piece(k3, step)) - row_max[:, :, None]), axis=-1)

    row_total = lax.psum(lax.fori_loop(0, nblk, total_step, zeros), "mem")

    def attend_step(step, acc):
        probs = weights(scored(q3, piece(k3, step)), row_max, row_total)
        return acc + jnp.einsum(
            "hrj,jhd->rhd", probs, piece(v3, step), preferred_element_type=jnp.float32
        )

    attended = lax.fori_loop(0, nblk, attend_step, jnp.zeros((rows, H, DH), jnp.float32))
    attended = lax.psum(attended, "mem")
    row_term = jnp.sum(do3.astype(jnp.float32) * attended, axis=-1).T
    all_queries, all_douts = (
        lax.all_gather(queries, "pb", axis=0, tiled=True),
        lax.all_gather(d_out, "pb", axis=0, tiled=True),
    )
    all_max, all_total, all_term = (
        lax.all_gather(row_max, "pb", axis=1, tiled=True),
        lax.all_gather(row_total, "pb", axis=1, tiled=True),
        lax.all_gather(row_term, "pb", axis=1, tiled=True),
    )
    every = all_queries.shape[0]
    share = slots // lax.axis_size("pb")
    start = lax.axis_index("pb") * share
    key_part = lax.dynamic_slice_in_dim(k3, start, share, 0)
    value_part = lax.dynamic_slice_in_dim(v3, start, share, 0)
    dq_full, dk_own, dv_own = grads(
        all_queries.reshape(every, H, DH),
        all_douts.reshape(every, H, DH),
        all_max,
        all_total,
        all_term,
        key_part,
        value_part,
    )
    dq_own = lax.psum_scatter(
        dq_full.reshape(every, H * DH), ("pb", "mem"), scatter_dimension=0, tiled=True
    )
    dk_own = dk_own.reshape(share, H * DH)
    dv_own = dv_own.reshape(share, H * DH)
    query_grad = scale * dq_own
    key_grad = (scale * dk_own).astype(jnp.bfloat16).reshape(1, share, H * DH)
    value_grad = dv_own.astype(jnp.bfloat16).reshape(1, share, H * DH)
    return (query_grad, key_grad, value_grad)


def solution(mesh):
    return jax.shard_map(
        shards,
        mesh=mesh,
        in_specs=(P("pb", None), P("mem", None), P("mem", None), P("pb", None)),
        out_specs=(P(("pb", "mem"), None), P("mem", "pb", None), P("mem", "pb", None)),
        check_vma=False,
    )
```

profile of v0, /device:TPU:1, one launch (start us, length us, event | category | flops | bytes accessed | tf_op | source)
XLA Modules:
  0.0 1877.0 jit_solution(2811855088350916889)
XLA Ops:
  8.1 1.5 copy_bitcast_fusion
  9.6 1.5 copy.45
  11.0 6.4 copy.18
  17.4 6.4 copy.19
  23.8 5.8 while.42
  23.8 2.9 multiply_reduce_fusion.3
  26.7 2.9 multiply_reduce_fusion.3
  29.6 107.7 %pmax.7 = f32[16,256]{1,0:T(8,128)S(1)} all-reduce(f32[16,256]{1,0:T(8,128)S(1)} %get-tuple-element.300), channel_id=1, replica_groups=mesh['pb'=8,'mem'=32] {'mem'}, use_global_device_ids=true, to_apply=%region_3.0 | all-reduce | flops 4096 | bytes 32768 | tf_op jit(solution)/shard_map/pmax | solution.py:48
  137.3 6.5 while.43
  137.4 3.2 exponential_reduce_fusion.2
  140.6 3.2 exponential_reduce_fusion.2
  143.8 104.4 %psum.14 = f32[16,256]{1,0:T(8,128)S(1)} all-reduce(f32[16,256]{1,0:T(8,128)S(1)} %get-tuple-element.301), channel_id=1, replica_groups=mesh['pb'=8,'mem'=32] {'mem'}, use_global_device_ids=true, to_apply=%region_7.0 | all-reduce | flops 4096 | bytes 32768 | tf_op jit(solution)/shard_map/psum | solution.py:53
  248.2 6.4 copy.26
  254.6 13.2 while.44
  254.6 6.3 bitcast_add_fusion.2
  261.0 6.8 bitcast_add_fusion.2
  267.9 1.3 copy.20
  269.3 1.3 copy.28
  271.2 28.4 %all_gather.17 = f32[16,2048]{1,0:T(8,128)S(1)} all-gather(f32[16,256]{1,0:T(8,128)S(1)} %get-tuple-element.633), channel_id=1, replica_groups=mesh['pb'=8,'mem'=32] {'pb'}, dimensions={1}, use_global_device_ids=true | all-gather | bytes 147456 | tf_op jit(solution)/shard_map/all_gather | solution.py:70
  299.6 28.0 %all_gather.16 = f32[16,2048]{1,0:T(8,128)S(1)} all-gather(f32[16,256]{1,0:T(8,128)S(1)} %get-tuple-element.632), channel_id=1, replica_groups=mesh['pb'=8,'mem'=32] {'pb'}, dimensions={1}, use_global_device_ids=true | all-gather | bytes 147456 | tf_op jit(solution)/shard_map/all_gather | solution.py:69
  327.6 173.3 %all-reduce.2.cloned.1.call-done = f32[256,16,128]{0,2,1:T(8,128)} async-done(((f32[256,16,128]{0,2,1:T(8,128)}), f32[256,16,128]{0,2,1:T(8,128)}) %all-reduce.2.cloned.1.call-update) | async-done | bytes 2097168 | tf_op jit(solution)/shard_map/psum | solution.py:62
  500.9 1.9 multiply_reduce_fusion.1
  502.8 30.0 %all_gather.19 = f32[16,2048]{1,0:T(8,128)S(1)} all-gather(f32[16,256]{1,0:T(8,128)S(1)} %bitcast.50), channel_id=1, replica_groups=mesh['pb'=8,'mem'=32] {'pb'}, dimensions={1}, use_global_device_ids=true | all-gather | bytes 147456 | tf_op jit(solution)/shard_map/all_gather | solution.py:71
  532.9 9.2 divide_convert_fusion.4
  542.0 8.9 multiply_convert_fusion
  550.9 9.5 fusion.21
  560.5 17.6 copy.33
  578.1 8.1 fusion.19
  586.2 1.0 copy.34
  587.2 8.2 convolution_convert_fusion
  596.4 1271.7 %reduce-scatter.2.cloned.1.call-done = f32[8,2048]{1,0:T(8,128)} async-done(((f32[2048,2048]{1,0:T(8,128)}), f32[8,2048]{1,0:T(8,128)}) %reduce-scatter.2.cloned.1.call-update) | async-done | bytes 65552 | tf_op jit(solution)/shard_map/reduce_scatter | solution.py:87
  1868.1 1.5 broadcast_multiply_fusion
  (25 shorter events, 1.8 us)
Async XLA Ops:
  8.0 492.9 %all-reduce.2.cloned.1.call-start = ((), (), s32[]{:S(2)}) async-start(), calls=%async_computation.3 | async-start | bytes 4194304 | tf_op jit(solution)/shard_map/psum | solution.py:62
  254.6 13.2 copy-start.1
  254.6 14.7 copy-start.2
  267.8 265.1 %all-gather.3.cloned.1.call-start = ((), (), s32[]{:S(2)}) async-start(), calls=%async_computation.1 | async-start | bytes 9437184 | tf_op jit(solution)/shard_map/all_gather | solution.py:65
  269.2 272.8 %all-gather.5.cloned.1.call-start = ((), (), s32[]{:S(2)}) async-start(), calls=%async_computation.2 | async-start | bytes 9437184 | tf_op jit(solution)/shard_map/all_gather | solution.py:66
  270.6 1597.4 %reduce-scatter.2.cloned.1.call-start = ((), (), s32[]{:S(2)}) async-start(), calls=%async_computation.4 | async-start | bytes 16842752 | tf_op jit(solution)/shard_map/reduce_scatter | solution.py:87
  550.9 9.6 copy-start
Sparse Core Ops, SparseCore 0:
  267.9 232.9 all-reduce.1
  578.2 1289.7 reduce-scatter.1
Sparse Core Ops, SparseCore 1:
  271.1 129.5 all-gather.2
  403.3 128.6 all-gather.4
where the time goes:
time: 1880 us
  waiting for transfers between devices  1450 us (77%)
  blocking collectives  299 us (16%)
  matrix products  69.1 us (4%)
  local copies, waits for them, and re-layouts  44.9 us (2%)
    reduce_scatter x1, waiting for transfers between devices, shards(): lax.psum_scatter(dq_full.reshape(every, H * DH), ('pb', 'mem'), scatter_d...  1270 us
    psum x1, waiting for transfers between devices, shards(): attended = lax.psum(attended, 'mem')  173 us
    pmax x1, blocking collectives, shards(): row_max = lax.pmax(lax.fori_loop(0, nblk, max_step, lowest), 'mem')  108 us
    psum x1, blocking collectives, shards(): row_total = lax.psum(lax.fori_loop(0, nblk, total_step, zeros), 'mem')  104 us
  transfers between devices with their start and end apart: 4, of which 2 were waited for; matrix products, arithmetic and copies ran while one was open for 2% of the time, Pallas kernels for 0%

commit v1 on v0

v1 whole, which is shorter than its diff:
```python
import functools
import math

import jax
import jax.numpy as jnp
from jax import lax
from jax.experimental import pallas as pl
from jax.experimental.pallas import tpu as pltpu
from jax.sharding import PartitionSpec as P

MESH = pl.DeviceIdType.MESH
DH = 128
NB = 8
NG = 16
RB = 256
KB = 1024
KP = 128
KT = 256
SCALE = DH ** -0.5
C2 = SCALE * math.log2(math.e)
F32 = jnp.float32
BF16 = jnp.bfloat16


def kernel(
    q_hbm, k_hbm, v_hbm, do_hbm, dq_out, dk_out, dv_out,
    qb, dob, kb, vb, kt, sc, dp, st, sr, rs, rr, dka, dva, dks, dvs, dqa, dqs, dqr, dqo,
    l_sem, kv_send, kv_recv, in_send, in_recv, st_send, st_recv, bc_send, bc_recv,
    o_send, o_recv, dq_send, dq_recv, f_send, f_recv,
):
    p = lax.axis_index("pb")
    m = lax.axis_index("mem")
    yh, x = p // 4, p % 4
    g, c = m // 2, m % 2
    head = 2 * p + c

    def cols(h):
        return pl.ds(pl.multiple_of(h * DH, DH), DH)

    def source(r):
        return (yh + r // 4) % 2 * 4 + (x + r) % 4

    def target(r):
        return (yh + r // 4) % 2 * 4 + (x + 4 - r % 4) % 4

    def local(src, dst, sem):
        pltpu.make_async_copy(src, dst, sem).start()

    def remote(src, dst, send, recv, pb, mem):
        pltpu.make_async_remote_copy(
            src_ref=src, dst_ref=dst, send_sem=send, recv_sem=recv,
            device_id=(pb, mem), device_id_type=MESH,
        ).start()

    def settle(ref, sem):
        pltpu.make_async_copy(ref, ref, sem).wait()

    local(k_hbm.at[:, cols(head)], kb.at[0], l_sem.at[0])
    local(v_hbm.at[:, cols(head)], vb.at[0], l_sem.at[1])
    local(q_hbm.at[:, cols(head)], qb.at[0], in_recv.at[0, 0])
    local(do_hbm.at[:, cols(head)], dob.at[0], in_recv.at[0, 1])

    barrier = pltpu.get_barrier_semaphore()

    @pl.loop(1, 2 * NB)
    def _(i):
        pl.semaphore_signal(
            barrier, inc=1, device_id=((p + i // 2) % NB, 2 * g + (c + i) % 2), device_id_type=MESH
        )

    @pl.loop(1, NG)
    def _(i):
        pl.semaphore_signal(
            barrier, inc=1, device_id=(p, (g + i) % NG * 2 + c), device_id_type=MESH
        )

    pl.semaphore_wait(barrier, 2 * NB + NG - 2)

    mate = 2 * p + 1 - c
    remote(k_hbm.at[:, cols(mate)], kb.at[1], kv_send, kv_recv, p, 2 * g + 1 - c)
    remote(v_hbm.at[:, cols(mate)], vb.at[1], kv_send, kv_recv, p, 2 * g + 1 - c)

    @pl.loop(1, NB)
    def _(r):
        to = target(r)
        remote(q_hbm.at[:, cols(2 * to + c)], qb.at[r], in_send.at[0], in_recv.at[r, 0], to, m)
        remote(do_hbm.at[:, cols(2 * to + c)], dob.at[r], in_send.at[1], in_recv.at[r, 1], to, m)

    settle(kb.at[0], l_sem.at[0])
    settle(vb.at[0], l_sem.at[1])
    settle(kb, kv_recv)

    for half in range(2):
        kt[half] = kb[half].T

    def combine(tile):
        @pl.when(g // 2 == tile)
        def _():
            settle(sr, st_recv)
            tm, tl, tt = sr[:, 0, :], sr[:, 1, :], sr[:, 2, :]
            top = jnp.max(tm, axis=0, keepdims=True)
            w = jnp.exp2((tm - top) * C2)
            total = jnp.sum(tl * w, axis=0, keepdims=True)
            term = jnp.sum(tt * w, axis=0, keepdims=True) / total
            rs[...] = jnp.concatenate([top * C2 + jnp.log2(total), term, jnp.zeros((6, 128), F32)], axis=0)
            local(rs, rr.at[g], bc_recv.at[g])

            @pl.loop(1, NG)
            def _(i):
                remote(rs, rr.at[g], bc_send, bc_recv.at[g], p, (g + i) % NG * 2 + c)

    def forward(r, carry):
        settle(qb.at[r], in_recv.at[r, 0])
        settle(dob.at[r], in_recv.at[r, 1])
        q = qb[r]
        do = dob[r]
        top = jnp.full((8, RB), -1e30, F32)
        total = jnp.zeros((8, RB), F32)
        term = jnp.zeros((8, RB), F32)
        for half in range(2):
            for j in range(KB // KT):
                rows = pl.ds(j * KT, KT)
                s = lax.dot_general(kb[half, rows, :], q, (((1,), (1,)), ((), ())), preferred_element_type=F32)
                d = lax.dot_general(vb[half, rows, :], do, (((1,), (1,)), ((), ())), preferred_element_type=F32)
                sc[r, half, rows, :] = s
                dp[r, half, rows, :] = d
                s = s.reshape(KT // 8, 8, RB)
                d = d.reshape(KT // 8, 8, RB)
                new = jnp.maximum(top, jnp.max(s, axis=0))
                w = jnp.exp2((top - new) * C2)
                e = jnp.exp2((s - new[None]) * C2)
                total = total * w + jnp.sum(e, axis=0)
                term = term * w + jnp.sum(e * d, axis=0)
                top = new
        peak = jnp.max(top, axis=0, keepdims=True)
        w = jnp.exp2((top - peak) * C2)
        total = jnp.sum(total * w, axis=0, keepdims=True)
        term = jnp.sum(term * w, axis=0, keepdims=True)
        for k in range(2):
            lanes = slice(k * 128, k * 128 + 128)
            tile = 2 * r + k
            st[tile] = jnp.concatenate(
                [peak[:, lanes], total[:, lanes], term[:, lanes], jnp.zeros((5, 128), F32)], axis=0
            )

            @pl.when(g == tile)
            def _():
                local(st.at[tile], sr.at[g], st_recv)

            @pl.when(g != tile)
            def _():
                remote(st.at[tile], sr.at[g], st_send, st_recv, p, tile * 2 + c)

        combine(r - 2)
        return carry

    lax.fori_loop(0, NB, forward, 0)

    def backward(half, r):
        if half == 0:
            settle(rr.at[2 * r], bc_recv.at[2 * r])
            settle(rr.at[2 * r + 1], bc_recv.at[2 * r + 1])
        b = jnp.concatenate([rr[2 * r, 0:1, :], rr[2 * r + 1, 0:1, :]], axis=1)
        t = jnp.concatenate([rr[2 * r, 1:2, :], rr[2 * r + 1, 1:2, :]], axis=1)
        q = qb[r]
        do = dob[r]
        dq = jnp.zeros((DH, RB), F32)
        for j in range(KB // KT):
            rows = pl.ds(j * KT, KT)
            pr = jnp.exp2(sc[r, half, rows, :] * C2 - b)
            ds = (pr * (dp[r, half, rows, :] - t)).astype(BF16)
            pr = pr.astype(BF16)
            dva[rows, :] += jnp.dot(pr, do, preferred_element_type=F32)
            dka[rows, :] += jnp.dot(ds, q, preferred_element_type=F32)
            dq += jnp.dot(kt[half, :, rows], ds, preferred_element_type=F32)
        return dq

    def ship(half):
        dks[half * NB:(half + 1) * NB] = (dka[...] * SCALE).astype(BF16).reshape(NB, KP, DH)
        dvs[half * NB:(half + 1) * NB] = dva[...].astype(BF16).reshape(NB, KP, DH)
        to_c = 2 * g + (c + half) % 2
        if half == 0:
            local(dks.at[p], dk_out.at[:, cols(head)], o_recv.at[0])
            local(dvs.at[p], dv_out.at[:, cols(head)], o_recv.at[1])
        else:
            remote(dks.at[NB + p], dk_out.at[:, cols(head)], o_send.at[0], o_recv.at[0], p, to_c)
            remote(dvs.at[NB + p], dv_out.at[:, cols(head)], o_send.at[1], o_recv.at[1], p, to_c)

        @pl.loop(1, NB)
        def _(r):
            to = target(r)
            remote(dks.at[half * NB + to], dk_out.at[:, cols(head)], o_send.at[0], o_recv.at[0], to, to_c)
            remote(dvs.at[half * NB + to], dv_out.at[:, cols(head)], o_send.at[1], o_recv.at[1], to, to_c)

    dka[...] = jnp.zeros_like(dka)
    dva[...] = jnp.zeros_like(dva)

    def first(r, carry):
        dqa[r] = backward(0, r)
        combine(r + NB - 2)
        return carry

    lax.fori_loop(0, NB, first, 0)
    ship(0)
    dka[...] = jnp.zeros_like(dka)
    dva[...] = jnp.zeros_like(dva)

    def second(i, carry):
        for k in range(2):
            r = 2 * i + k
            dq = (backward(1, r) + dqa[r]) * SCALE
            dqs[i, :, k] = dq.T.astype(BF16).reshape(NG, RB // NG, DH)
        local(dqs.at[i, g], dqr.at[i, g], dq_recv.at[i])

        @pl.loop(1, NG)
        def _(n):
            to = (g + n) % NG
            remote(dqs.at[i, to], dqr.at[i, g], dq_send, dq_recv.at[i], p, to * 2 + c)

        return carry

    lax.fori_loop(0, NB // 2, second, 0)
    ship(1)

    for i in range(NB // 2):
        settle(dqr.at[i], dq_recv.at[i])
        for k in range(2):
            r = 2 * i + k
            acc = jnp.sum(dqr[i, :, k].astype(F32), axis=0)
            dqo[2 * r:2 * r + 2] = acc.reshape(2, 8, DH)
            to = source(r)
            for e in range(2):
                dst = dq_out.at[:, cols(head)]
                if r == 0 and e == 0:
                    local(dqo.at[c], dst, f_recv)
                else:
                    ce = (c + e) % 2
                    remote(dqo.at[2 * r + ce], dst, f_send, f_recv, to, 2 * g + ce)

    settle(dq_out, f_recv)
    settle(dk_out, o_recv.at[0])
    settle(dv_out, o_recv.at[1])
    settle(kb, kv_send)
    settle(qb.at[1:], in_send.at[0])
    settle(dob.at[1:], in_send.at[1])
    settle(st.at[1:], st_send)
    settle(rr.at[1:], bc_send)
    settle(dqs.at[:, 1:], dq_send)
    settle(dks.at[1:], o_send.at[0])
    settle(dvs.at[1:], o_send.at[1])
    settle(dqo.at[1:], f_send)


def shards(queries, keys, values, d_out):
    width = queries.shape[1]
    dma = pltpu.SemaphoreType.DMA
    return pl.pallas_call(
        kernel,
        out_shape=(
            jax.ShapeDtypeStruct((8, width), F32),
            jax.ShapeDtypeStruct((KP, width), BF16),
            jax.ShapeDtypeStruct((KP, width), BF16),
        ),
        in_specs=[pl.BlockSpec(memory_space=pl.ANY)] * 4,
        out_specs=[pl.BlockSpec(memory_space=pl.ANY)] * 3,
        scratch_shapes=[
            pltpu.VMEM((NB, RB, DH), BF16),
            pltpu.VMEM((NB, RB, DH), BF16),
            pltpu.VMEM((2, KB, DH), BF16),
            pltpu.VMEM((2, KB, DH), BF16),
            pltpu.VMEM((2, DH, KB), BF16),
            pltpu.VMEM((NB, 2, KB, RB), F32),
            pltpu.VMEM((NB, 2, KB, RB), F32),
            pltpu.VMEM((NG, 8, 128), F32),
            pltpu.VMEM((NG, 8, 128), F32),
            pltpu.VMEM((8, 128), F32),
            pltpu.VMEM((NG, 8, 128), F32),
            pltpu.VMEM((KB, DH), F32),
            pltpu.VMEM((KB, DH), F32),
            pltpu.VMEM((2 * NB, KP, DH), BF16),
            pltpu.VMEM((2 * NB, KP, DH), BF16),
            pltpu.VMEM((NB, DH, RB), F32),
            pltpu.VMEM((NB // 2, NG, 2, RB // NG, DH), BF16),
            pltpu.VMEM((NB // 2, NG, 2, RB // NG, DH), BF16),
            pltpu.VMEM((2 * NB, 8, DH), F32),
            dma((2,)),
            dma,
            dma,
            dma((2,)),
            dma((NB, 2)),
            dma,
            dma,
            dma,
            dma((NG,)),
            dma((2,)),
            dma((2,)),
            dma,
            dma((NB // 2,)),
            dma,
            dma,
        ],
        compiler_params=pltpu.CompilerParams(
            collective_id=0, has_side_effects=True, vmem_limit_bytes=56 * 2**20
        ),
        cost_estimate=pl.CostEstimate(flops=5 * 2 * 2048 * 2048 * 128, bytes_accessed=12 * 2**20, transcendentals=2 * 2048 * 2048),
    )(queries, keys, values, d_out)


def solution(mesh):
    def run(queries, keys, values, d_out):
        dq, dk, dv = shards(queries, keys, values, d_out)
        return dq, dk[None], dv[None]

    return jax.shard_map(
        run,
        mesh=mesh,
        in_specs=(P("pb", None), P("mem", None), P("mem", None), P("pb", None)),
        out_specs=(P(("pb", "mem"), None), P("mem", "pb", None), P("mem", "pb", None)),
        check_vma=False,
    )
```

time: 1880 us -> 68.2 us (0.04)
  waiting for transfers between devices: 1450 us -> 0 us
  blocking collectives: 299 us -> 0 us
  matrix products: 69.1 us -> 0 us
  Pallas kernels: 0 us -> 62.1 us
  local copies, waits for them, and re-layouts: 44.9 us -> 5.23 us
    reduce_scatter x1 -> x0, waiting for transfers between devices: 1270 us -> none  [shards(): lax.psum_scatter(dq_full.reshape(every, H * DH), ('pb', 'mem'), scatter_d...]
    psum x1 -> x0, waiting for transfers between devices: 173 us -> none  [shards(): attended = lax.psum(attended, 'mem')]
    pmax x1 -> x0, blocking collectives: 108 us -> none  [shards(): row_max = lax.pmax(lax.fori_loop(0, nblk, max_step, lowest), 'mem')]
    psum x1 -> x0, blocking collectives: 104 us -> none  [shards(): row_total = lax.psum(lax.fori_loop(0, nblk, total_step, zeros), 'mem')]
    all_gather x3 -> x0, blocking collectives: 86.5 us -> none  [the longest x1 30 us: shards(): lax.all_gather(row_term, 'pb', axis=1, tiled=True)]
    dot_general x11 -> x0, matrix products: 69.1 us -> none  [the longest x5 21.3 us: scored(): jnp.einsum('rhd,jhd->hrj', q3, kb, preferred_element_type=jnp.float32)]
    pallas_call x0 -> x1, Pallas kernels: none -> 62.1 us  [shards(): pl.pallas_call(kernel, out_shape=(jax.ShapeDtypeStruct((8, width), F32),...]
    reshape x2 -> x0, local copies, waits for them, and re-layouts: 24 us -> none  [the longest x1 17.6 us: shards(): dq_full.reshape(every, H * DH)]
  transfers between devices with their start and end apart: 4 -> 0, of which waited for: 2 -> 0; matrix products, arithmetic and copies ran while one was open for 2% -> 0% of each run, Pallas kernels for 0% -> 0%
where the time goes in v1:
time: 68.2 us; the launch traced here: 67.9 us
  Pallas kernels  62.1 us (91%)
  local copies, waits for them, and re-layouts  5.23 us (8%)
    pallas_call x1, Pallas kernels, shards(): pl.pallas_call(kernel, out_shape=(jax.ShapeDtypeStruct((8, width), F32),...  62.1 us
    unnamed x3, local copies, waits for them, and re-layouts  5.23 us

profile of v1, /device:TPU:1, one launch (start us, length us, event | category | flops | bytes accessed | tf_op | source)
XLA Modules:
  0.0 67.9 jit_solution(10927889898858031370)
XLA Ops:
  0.6 62.1 %shard_map.67 = (f32[8,2048]{1,0:T(8,128)}, bf16[128,2048]{1,0:T(8,128)(2,1)}, bf16[128,2048]{1,0:T(8,128)(2,1)}) custom-call(bf16[256,2048]{1,0:T(8,128)(2,1)} %q_hbm.1, bf16[1024,2048]{1,0:T(8,128)(2,1)} %k_hbm.1, bf16[1024,2048]{1,0:T(8,128)(2,1)} %v_hbm.1, bf16[256,2048]{1,0:T(8,128)(2,1)} %do_hbm.1), custom_call_target="tpu_custom_call" | custom-call | flops 5368709120 | bytes 12582912 | tf_op jit(solution)/shard_map/pallas_call | solution.py:257
  62.7 1.5 %copy.10 = f32[8,2048]{1,0:T(8,128)} copy(f32[8,2048]{1,0:T(8,128)} %get-tuple-element.12) | data formatting | bytes 131072
  64.2 1.9 %copy.11 = bf16[1,128,2048]{2,1,0:T(8,128)(2,1)} copy(bf16[1,128,2048]{2,1,0:T(8,128)(2,1)} %bitcast.3) | data formatting | bytes 1048576
  66.1 1.9 %copy.12 = bf16[1,128,2048]{2,1,0:T(8,128)(2,1)} copy(bf16[1,128,2048]{2,1,0:T(8,128)(2,1)} %bitcast.2) | data formatting | bytes 1048576

commit v2 on v1

v2 whole, which is shorter than its diff:
```python
import functools
import math

import jax
import jax.numpy as jnp
from jax import lax
from jax.experimental import pallas as pl
from jax.experimental.pallas import tpu as pltpu
from jax.sharding import PartitionSpec as P

MESH = pl.DeviceIdType.MESH
DH = 128
NB = 8
NG = 16
RB = 256
KB = 1024
KP = 128
KT = 256
LAG = 2
BATCH = 2
ORDER = (0, 1, 3, 4, 2, 5, 7, 6)
SCALE = DH ** -0.5
C2 = SCALE * math.log2(math.e)
F32 = jnp.float32
BF16 = jnp.bfloat16


def kernel(
    q_hbm, k_hbm, v_hbm, do_hbm, dq_out, dk_out, dv_out,
    qb, dob, kb, vb, kt, sc, dp, st, sr, dka, dva, dks, dvs, dqs, dqr, dqo,
    l_sem, kv_send, kv_recv, in_send, in_recv, st_send, st_recv,
    o_send, o_recv, dq_send, dq_recv, f_send, f_recv,
):
    p = lax.axis_index("pb")
    m = lax.axis_index("mem")
    g, c = m // 2, m % 2
    head = 2 * p + c

    def cols(h):
        return pl.ds(pl.multiple_of(h * DH, DH), DH)

    def local(src, dst, sem):
        pltpu.make_async_copy(src, dst, sem).start()

    def remote(src, dst, send, recv, pb, mem):
        pltpu.make_async_remote_copy(
            src_ref=src, dst_ref=dst, send_sem=send, recv_sem=recv,
            device_id=(pb, mem), device_id_type=MESH,
        ).start()

    def settle(ref, sem):
        pltpu.make_async_copy(ref, ref, sem).wait()

    local(k_hbm.at[:, cols(head)], kb.at[0], l_sem.at[0])
    local(v_hbm.at[:, cols(head)], vb.at[0], l_sem.at[1])
    local(q_hbm.at[:, cols(head)], qb.at[0], in_recv.at[0, 0])
    local(do_hbm.at[:, cols(head)], dob.at[0], in_recv.at[0, 1])

    barrier = pltpu.get_barrier_semaphore()
    for i in range(1, 2 * NB):
        pl.semaphore_signal(barrier, inc=1, device_id=(p ^ (i >> 1), m ^ (i & 1)), device_id_type=MESH)
    for i in range(1, NG):
        pl.semaphore_signal(barrier, inc=1, device_id=(p, m ^ (2 * i)), device_id_type=MESH)
    pl.semaphore_wait(barrier, 2 * NB + NG - 2)

    mate = 2 * p + 1 - c
    remote(k_hbm.at[:, cols(mate)], kb.at[1], kv_send, kv_recv, p, m ^ 1)
    remote(v_hbm.at[:, cols(mate)], vb.at[1], kv_send, kv_recv, p, m ^ 1)
    for i in range(1, NB):
        to = p ^ ORDER[i]
        remote(q_hbm.at[:, cols(2 * to + c)], qb.at[i], in_send.at[0], in_recv.at[i, 0], to, m)
        remote(do_hbm.at[:, cols(2 * to + c)], dob.at[i], in_send.at[1], in_recv.at[i, 1], to, m)

    dka[...] = jnp.zeros_like(dka)
    dva[...] = jnp.zeros_like(dva)
    settle(kb.at[0], l_sem.at[0])
    settle(vb.at[0], l_sem.at[1])
    settle(kb, kv_recv)
    for half in range(2):
        kt[half] = kb[half].T

    def forward(r):
        settle(qb.at[r], in_recv.at[r, 0])
        settle(dob.at[r], in_recv.at[r, 1])
        q = qb[r]
        do = dob[r]
        top = jnp.full((8, RB), -1e30, F32)
        total = jnp.zeros((8, RB), F32)
        term = jnp.zeros((8, RB), F32)
        for half in range(2):
            for j in range(KB // KT):
                rows = pl.ds(j * KT, KT)
                s = lax.dot_general(kb[half, rows, :], q, (((1,), (1,)), ((), ())), preferred_element_type=F32)
                d = lax.dot_general(vb[half, rows, :], do, (((1,), (1,)), ((), ())), preferred_element_type=F32)
                sc[r, half, rows, :] = s
                dp[r, half, rows, :] = d
                s = s.reshape(KT // 8, 8, RB)
                d = d.reshape(KT // 8, 8, RB)
                new = jnp.maximum(top, jnp.max(s, axis=0))
                w = jnp.exp2((top - new) * C2)
                e = jnp.exp2((s - new[None]) * C2)
                total = total * w + jnp.sum(e, axis=0)
                term = term * w + jnp.sum(e * d, axis=0)
                top = new
        peak = jnp.max(top, axis=0, keepdims=True)
        w = jnp.exp2((top - peak) * C2)
        total = jnp.sum(total * w, axis=0, keepdims=True)
        term = jnp.sum(term * w, axis=0, keepdims=True)
        tiles = [v[:, k * 128:k * 128 + 128] for v in (peak, total, term) for k in range(2)]
        st[r] = jnp.concatenate(tiles + [jnp.zeros((2, 128), F32)], axis=0)

    def send_stats(i):
        pair = pl.ds(2 * i, 2)
        local(st.at[pair], sr.at[i, g], st_recv.at[i])
        for n in range(1, NG):
            remote(st.at[pair], sr.at[i, g], st_send, st_recv.at[i], p, m ^ (2 * n))

    def stats(i, k):
        part = sr[i, :, k]
        tm, tl, tt = part[:, 0:2], part[:, 2:4], part[:, 4:6]
        top = jnp.max(tm, axis=0)
        w = jnp.exp2((tm - top) * C2)
        total = jnp.sum(tl * w, axis=0)
        t = jnp.sum(tt * w, axis=0) / total
        b = top * C2 + jnp.log2(total)
        return (jnp.concatenate([v[0:1], v[1:2]], axis=1) for v in (b, t))

    def piece(r, half, rows, b, t):
        pr = jnp.exp2(sc[r, half, rows, :] * C2 - b)
        ds = (pr * (dp[r, half, rows, :] - t)).astype(BF16)
        dv = jnp.dot(pr.astype(BF16), dob[r], preferred_element_type=F32)
        dk = jnp.dot(ds, qb[r], preferred_element_type=F32)
        dq = jnp.dot(kt[half, :, rows], ds, preferred_element_type=F32)
        return dk, dv, dq

    def send_dq(r, dq):
        batch, k = r // BATCH, r % BATCH
        dqs[batch, :, k] = (dq * SCALE).T.astype(BF16).reshape(NG, RB // NG, DH)

        @pl.when(k == BATCH - 1)
        def _():
            local(dqs.at[batch, g], dqr.at[batch, g], dq_recv.at[batch])
            for i in range(1, NG):
                remote(dqs.at[batch, g ^ i], dqr.at[batch, g], dq_send, dq_recv.at[batch], p, m ^ (2 * i))

    def backward(i, k):
        r = 2 * i + k
        b, t = stats(i, k)
        dq = jnp.zeros((DH, RB), F32)
        for half in range(2):
            for j in range(KB // KT):
                rows = pl.ds(j * KT, KT)
                dk, dv, part = piece(r, half, rows, b, t)
                dka[half, rows, :] += dk
                dva[half, rows, :] += dv
                dq += part
        send_dq(r, dq)

    def backward_last():
        r = NB - 1
        b, t = stats(NB // 2 - 1, 1)
        dq = jnp.zeros((DH, RB), F32)
        for e in range(KB // KT):
            for half in range(2):
                j = (p >> 1) ^ (KB // KT - 1 - e)
                rows = pl.ds(pl.multiple_of(j * KT, KT), KT)
                dk, dv, part = piece(r, half, rows, b, t)
                dk = ((dka[half, rows, :] + dk) * SCALE).astype(BF16)
                dv = (dva[half, rows, :] + dv).astype(BF16)
                dq += part
                dks[pl.ds(half * NB + 2 * j, 2)] = dk.reshape(2, KP, DH)
                dvs[pl.ds(half * NB + 2 * j, 2)] = dv.reshape(2, KP, DH)
                for n in range(2):
                    to = p ^ (2 * (KB // KT - 1 - e) + 1 - n)
                    for ref, out, i in ((dks, dk_out, 0), (dvs, dv_out, 1)):
                        if half == 0 and e == KB // KT - 1 and n == 1:
                            local(ref.at[to], out.at[:, cols(head)], o_recv.at[i])
                        else:
                            remote(ref.at[half * NB + to], out.at[:, cols(head)], o_send.at[i], o_recv.at[i], to, m ^ half)
        send_dq(r, dq)

    def lead(i, carry):
        forward(2 * i)
        forward(2 * i + 1)
        send_stats(i)
        return carry

    def steady(i, carry):
        lead(i, carry)
        return rest(i - LAG, carry)

    def rest(i, carry):
        settle(sr.at[i], st_recv.at[i])
        backward(i, 0)
        backward(i, 1)
        return carry

    lax.fori_loop(0, LAG, lead, 0)
    lax.fori_loop(LAG, NB // 2, steady, 0)
    lax.fori_loop(NB // 2 - LAG, NB // 2 - 1, rest, 0)
    settle(sr.at[NB // 2 - 1], st_recv.at[NB // 2 - 1])
    backward(NB // 2 - 1, 0)
    backward_last()

    for batch in range(NB // BATCH):
        settle(dqr.at[batch], dq_recv.at[batch])
        for k in range(BATCH):
            r = batch * BATCH + k
            acc = jnp.sum(dqr[batch, :, k].astype(F32), axis=0)
            dqo[2 * r:2 * r + 2] = acc.reshape(2, 8, DH)
            to = p ^ ORDER[r]
            for e in range(2):
                dst = dq_out.at[:, cols(head)]
                if r == 0 and e == 0:
                    local(dqo.at[c], dst, f_recv)
                else:
                    remote(dqo.at[2 * r + (c ^ e)], dst, f_send, f_recv, to, m ^ e)

    settle(kb, kv_send)
    settle(qb.at[1:], in_send.at[0])
    settle(dob.at[1:], in_send.at[1])
    settle(sr.at[:, 1:], st_send)
    settle(dqs.at[:, 1:], dq_send)
    settle(dqo.at[1:], f_send)
    settle(dks.at[1:], o_send.at[0])
    settle(dvs.at[1:], o_send.at[1])
    settle(dq_out, f_recv)
    settle(dk_out, o_recv.at[0])
    settle(dv_out, o_recv.at[1])


def place(dq, dk, dv, dq_out, dk_out, dv_out, dqv, dkv, dvv, in_sem, out_sem):
    steps = [(dq, dqv, dq_out)]
    for n in range(2):
        rows = pl.ds(n * KP // 2, KP // 2)
        for src, via, dst in ((dk, dkv, dk_out.at[0]), (dv, dvv, dv_out.at[0])):
            steps.append((src.at[rows], via.at[rows], dst.at[rows]))
    fetch = [pltpu.make_async_copy(src, via, in_sem.at[i]) for i, (src, via, _) in enumerate(steps)]
    store = [pltpu.make_async_copy(via, dst, out_sem.at[i]) for i, (_, via, dst) in enumerate(steps)]
    for copy in fetch:
        copy.start()
    for first, second in zip(fetch, store):
        first.wait()
        second.start()
    for copy in store:
        copy.wait()


def shards(queries, keys, values, d_out):
    width = queries.shape[1]
    dma = pltpu.SemaphoreType.DMA
    any_space = pl.BlockSpec(memory_space=pl.ANY)
    dq, dk, dv = pl.pallas_call(
        kernel,
        out_shape=(
            jax.ShapeDtypeStruct((8, width), F32),
            jax.ShapeDtypeStruct((KP, width), BF16),
            jax.ShapeDtypeStruct((KP, width), BF16),
        ),
        in_specs=[any_space] * 4,
        out_specs=[any_space] * 3,
        scratch_shapes=[
            pltpu.VMEM((NB, RB, DH), BF16),
            pltpu.VMEM((NB, RB, DH), BF16),
            pltpu.VMEM((2, KB, DH), BF16),
            pltpu.VMEM((2, KB, DH), BF16),
            pltpu.VMEM((2, DH, KB), BF16),
            pltpu.VMEM((NB, 2, KB, RB), F32),
            pltpu.VMEM((NB, 2, KB, RB), F32),
            pltpu.VMEM((NB, 8, 128), F32),
            pltpu.VMEM((NB // 2, NG, 2, 8, 128), F32),
            pltpu.VMEM((2, KB, DH), F32),
            pltpu.VMEM((2, KB, DH), F32),
            pltpu.VMEM((2 * NB, KP, DH), BF16),
            pltpu.VMEM((2 * NB, KP, DH), BF16),
            pltpu.VMEM((NB // BATCH, NG, BATCH, RB // NG, DH), BF16),
            pltpu.VMEM((NB // BATCH, NG, BATCH, RB // NG, DH), BF16),
            pltpu.VMEM((2 * NB, 8, DH), F32),
            dma((2,)),
            dma,
            dma,
            dma((2,)),
            dma((NB, 2)),
            dma,
            dma((NB // 2,)),
            dma((2,)),
            dma((2,)),
            dma,
            dma((NB // BATCH,)),
            dma,
            dma,
        ],
        compiler_params=pltpu.CompilerParams(
            collective_id=0, has_side_effects=True, vmem_limit_bytes=56 * 2**20
        ),
        cost_estimate=pl.CostEstimate(flops=5 * 2 * 2048 * 2048 * 128, bytes_accessed=12 * 2**20, transcendentals=2 * 2048 * 2048),
    )(queries, keys, values, d_out)
    return pl.pallas_call(
        place,
        out_shape=(
            jax.ShapeDtypeStruct((8, width), F32),
            jax.ShapeDtypeStruct((1, KP, width), BF16),
            jax.ShapeDtypeStruct((1, KP, width), BF16),
        ),
        in_specs=[any_space] * 3,
        out_specs=[any_space] * 3,
        scratch_shapes=[
            pltpu.VMEM((8, width), F32),
            pltpu.VMEM((KP, width), BF16),
            pltpu.VMEM((KP, width), BF16),
            dma((5,)),
            dma((5,)),
        ],
    )(dq, dk, dv)


def solution(mesh):
    return jax.shard_map(
        shards,
        mesh=mesh,
        in_specs=(P("pb", None), P("mem", None), P("mem", None), P("pb", None)),
        out_specs=(P(("pb", "mem"), None), P("mem", "pb", None), P("mem", "pb", None)),
        check_vma=False,
    )
```

time: 68.2 us -> 61.9 us (0.908)
  local copies, waits for them, and re-layouts: 5.23 us -> 0 us
  Pallas kernels: 62.1 us -> 61.2 us
    unnamed x3 -> x0, local copies, waits for them, and re-layouts: 5.23 us -> none
    pallas_call x1, Pallas kernels: 62.1 us -> 59.1 us  [shards(): pl.pallas_call(kernel, out_shape=(jax.ShapeDtypeStruct((8, width), F32),...]
    pallas_call x0 -> x1, Pallas kernels: none -> 2.04 us  [shards(): pl.pallas_call(place, out_shape=(jax.ShapeDtypeStruct((8, width), F32), j...]
where the time goes in v2:
time: 61.9 us; the launch traced here: 61.8 us
  Pallas kernels  61.2 us (99%)
  between operations  0.64 us (1%)
    pallas_call x1, Pallas kernels, shards(): pl.pallas_call(kernel, out_shape=(jax.ShapeDtypeStruct((8, width), F32),...  59.1 us
    pallas_call x1, Pallas kernels, shards(): pl.pallas_call(place, out_shape=(jax.ShapeDtypeStruct((8, width), F32), j...  2.04 us

profile of v2, /device:TPU:1, one launch (start us, length us, event | category | flops | bytes accessed | tf_op | source)
XLA Modules:
  0.0 61.8 jit_solution(4762174980581731696)
XLA Ops:
  0.6 59.1 %shard_map.67 = (f32[8,2048]{1,0:T(8,128)}, bf16[128,2048]{1,0:T(8,128)(2,1)}, bf16[128,2048]{1,0:T(8,128)(2,1)}) custom-call(bf16[256,2048]{1,0:T(8,128)(2,1)} %q_hbm.1, bf16[1024,2048]{1,0:T(8,128)(2,1)} %k_hbm.1, bf16[1024,2048]{1,0:T(8,128)(2,1)} %v_hbm.1, bf16[256,2048]{1,0:T(8,128)(2,1)} %do_hbm.1), custom_call_target="tpu_custom_call" | custom-call | flops 5368709120 | bytes 12582912 | tf_op jit(solution)/shard_map/pallas_call | solution.py:253
  59.8 2.0 %shard_map.68 = (f32[8,2048]{1,0:T(8,128)}, bf16[1,128,2048]{2,1,0:T(8,128)(2,1)}, bf16[1,128,2048]{2,1,0:T(8,128)(2,1)}) custom-call(f32[8,2048]{1,0:T(8,128)} %get-tuple-element.6.dq, bf16[128,2048]{1,0:T(8,128)(2,1)} %get-tuple-element.7.dk, bf16[128,2048]{1,0:T(8,128)(2,1)} %get-tuple-element.8.dv), custom_call_target="tpu_custom_call" | custom-call | tf_op jit(solution)/shard_map/pallas_call | solution.py:298

commit v3 on v2

--- a/solution.py
+++ b/solution.py
@@ -16,9 +16,11 @@
 KB = 1024
 KP = 128
 KT = 256
-LAG = 2
+LAG = 3
 BATCH = 2
-ORDER = (0, 1, 3, 4, 2, 5, 7, 6)
+ORDER = (0, 6, 7, 5, 2, 4, 3, 1)
+EARLY = 0
+HELD = (0,)
 SCALE = DH ** -0.5
 C2 = SCALE * math.log2(math.e)
 F32 = jnp.float32
@@ -27,7 +29,7 @@
 
 def kernel(
     q_hbm, k_hbm, v_hbm, do_hbm, dq_out, dk_out, dv_out,
-    qb, dob, kb, vb, kt, sc, dp, st, sr, dka, dva, dks, dvs, dqs, dqr, dqo,
+    qb, dob, kb, vb, kt, sc, dp, st, sr, lp, ld, dka, dva, dks, dvs, dqs, dqr, dqo,
     l_sem, kv_send, kv_recv, in_send, in_recv, st_send, st_recv,
     o_send, o_recv, dq_send, dq_recv, f_send, f_recv,
 ):
@@ -61,47 +63,39 @@
         pl.semaphore_signal(barrier, inc=1, device_id=(p ^ (i >> 1), m ^ (i & 1)), device_id_type=MESH)
     for i in range(1, NG):
         pl.semaphore_signal(barrier, inc=1, device_id=(p, m ^ (2 * i)), device_id_type=MESH)
-    pl.semaphore_wait(barrier, 2 * NB + NG - 2)
-
-    mate = 2 * p + 1 - c
-    remote(k_hbm.at[:, cols(mate)], kb.at[1], kv_send, kv_recv, p, m ^ 1)
-    remote(v_hbm.at[:, cols(mate)], vb.at[1], kv_send, kv_recv, p, m ^ 1)
-    for i in range(1, NB):
-        to = p ^ ORDER[i]
-        remote(q_hbm.at[:, cols(2 * to + c)], qb.at[i], in_send.at[0], in_recv.at[i, 0], to, m)
-        remote(do_hbm.at[:, cols(2 * to + c)], dob.at[i], in_send.at[1], in_recv.at[i, 1], to, m)
-
-    dka[...] = jnp.zeros_like(dka)
-    dva[...] = jnp.zeros_like(dva)
-    settle(kb.at[0], l_sem.at[0])
-    settle(vb.at[0], l_sem.at[1])
-    settle(kb, kv_recv)
-    for half in range(2):
-        kt[half] = kb[half].T
-
-    def forward(r):
+    def score(r, half, state):
+        q = qb[r]
+        do = dob[r]
+        top, total, term = state
+        for j in range(KB // KT):
+            rows = pl.ds(j * KT, KT)
+            s = lax.dot_general(kb[half, rows, :], q, (((1,), (1,)), ((), ())), preferred_element_type=F32)
+            d = lax.dot_general(vb[half, rows, :], do, (((1,), (1,)), ((), ())), preferred_element_type=F32)
+            sc[r, half, rows, :] = s
+            dp[r, half, rows, :] = d
+            s = s.reshape(KT // 8, 8, RB)
+            d = d.reshape(KT // 8, 8, RB)
+            new = jnp.maximum(top, jnp.max(s, axis=0))
+            w = jnp.exp2((top - new) * C2)
+            e = jnp.exp2((s - new[None]) * C2)
+            total = total * w + jnp.sum(e, axis=0)
+            term = term * w + jnp.sum(e * d, axis=0)
+            top = new
+        return top, total, term
+
+    def fresh():
+        return jnp.full((8, RB), -1e30, F32), jnp.zeros((8, RB), F32), jnp.zeros((8, RB), F32)
+
+    def settle_in(r):
         settle(qb.at[r], in_recv.at[r, 0])
         settle(dob.at[r], in_recv.at[r, 1])
-        q = qb[r]
-        do = dob[r]
-        top = jnp.full((8, RB), -1e30, F32)
-        total = jnp.zeros((8, RB), F32)
-        term = jnp.zeros((8, RB), F32)
-        for half in range(2):
-            for j in range(KB // KT):
-                rows = pl.ds(j * KT, KT)
-                s = lax.dot_general(kb[half, rows, :], q, (((1,), (1,)), ((), ())), preferred_element_type=F32)
-                d = lax.dot_general(vb[half, rows, :], do, (((1,), (1,)), ((), ())), preferred_element_type=F32)
-                sc[r, half, rows, :] = s
-                dp[r, half, rows, :] = d
-                s = s.reshape(KT // 8, 8, RB)
-                d = d.reshape(KT // 8, 8, RB)
-                new = jnp.maximum(top, jnp.max(s, axis=0))
-                w = jnp.exp2((top - new) * C2)
-                e = jnp.exp2((s - new[None]) * C2)
-                total = total * w + jnp.sum(e, axis=0)
-                term = term * w + jnp.sum(e * d, axis=0)
-                top = new
+
+    def forward(r):
+        settle_in(r)
+        finish(r, score(r, 1, score(r, 0, fresh())))
+
+    def finish(r, state):
+        top, total, term = state
         peak = jnp.max(top, axis=0, keepdims=True)
         w = jnp.exp2((top - peak) * C2)
         total = jnp.sum(total * w, axis=0, keepdims=True)
@@ -125,10 +119,14 @@
         b = top * C2 + jnp.log2(total)
         return (jnp.concatenate([v[0:1], v[1:2]], axis=1) for v in (b, t))
 
-    def piece(r, half, rows, b, t):
+    def weigh(r, half, rows, b, t):
         pr = jnp.exp2(sc[r, half, rows, :] * C2 - b)
         ds = (pr * (dp[r, half, rows, :] - t)).astype(BF16)
-        dv = jnp.dot(pr.astype(BF16), dob[r], preferred_element_type=F32)
+        return pr.astype(BF16), ds
+
+    def piece(r, half, rows, b, t):
+        pr, ds = weigh(r, half, rows, b, t)
+        dv = jnp.dot(pr, dob[r], preferred_element_type=F32)
         dk = jnp.dot(ds, qb[r], preferred_element_type=F32)
         dq = jnp.dot(kt[half, :, rows], ds, preferred_element_type=F32)
         return dk, dv, dq
@@ -156,53 +154,7 @@
                 dq += part
         send_dq(r, dq)
 
-    def backward_last():
-        r = NB - 1
-        b, t = stats(NB // 2 - 1, 1)
-        dq = jnp.zeros((DH, RB), F32)
-        for e in range(KB // KT):
-            for half in range(2):
-                j = (p >> 1) ^ (KB // KT - 1 - e)
-                rows = pl.ds(pl.multiple_of(j * KT, KT), KT)
-                dk, dv, part = piece(r, half, rows, b, t)
-                dk = ((dka[half, rows, :] + dk) * SCALE).astype(BF16)
-                dv = (dva[half, rows, :] + dv).astype(BF16)
-                dq += part
-                dks[pl.ds(half * NB + 2 * j, 2)] = dk.reshape(2, KP, DH)
-                dvs[pl.ds(half * NB + 2 * j, 2)] = dv.reshape(2, KP, DH)
-                for n in range(2):
-                    to = p ^ (2 * (KB // KT - 1 - e) + 1 - n)
-                    for ref, out, i in ((dks, dk_out, 0), (dvs, dv_out, 1)):
-                        if half == 0 and e == KB // KT - 1 and n == 1:
-                            local(ref.at[to], out.at[:, cols(head)], o_recv.at[i])
-                        else:
-                            remote(ref.at[half * NB + to], out.at[:, cols(head)], o_send.at[i], o_recv.at[i], to, m ^ half)
-        send_dq(r, dq)
-
-    def lead(i, carry):
-        forward(2 * i)
-        forward(2 * i + 1)
-        send_stats(i)
-        return carry
-
-    def steady(i, carry):
-        lead(i, carry)
-        return rest(i - LAG, carry)
-
-    def rest(i, carry):
-        settle(sr.at[i], st_recv.at[i])
-        backward(i, 0)
-        backward(i, 1)
-        return carry
-
-    lax.fori_loop(0, LAG, lead, 0)
-    lax.fori_loop(LAG, NB // 2, steady, 0)
-    lax.fori_loop(NB // 2 - LAG, NB // 2 - 1, rest, 0)
-    settle(sr.at[NB // 2 - 1], st_recv.at[NB // 2 - 1])
-    backward(NB // 2 - 1, 0)
-    backward_last()
-
-    for batch in range(NB // BATCH):
+    def finals(batch):
         settle(dqr.at[batch], dq_recv.at[batch])
         for k in range(BATCH):
             r = batch * BATCH + k
@@ -215,6 +167,93 @@
                     local(dqo.at[c], dst, f_recv)
                 else:
                     remote(dqo.at[2 * r + (c ^ e)], dst, f_send, f_recv, to, m ^ e)
+
+    def ship(half, step):
+        to = p ^ step
+        for ref, out, i in ((dks, dk_out, 0), (dvs, dv_out, 1)):
+            if half == 0 and step == 0:
+                local(ref.at[to], out.at[:, cols(head)], o_recv.at[i])
+            else:
+                remote(ref.at[half * NB + to], out.at[:, cols(head)], o_send.at[i], o_recv.at[i], to, m ^ half)
+
+    def backward_last():
+        pair = NB // 2 - 1
+        for k in range(2):
+            r = 2 * pair + k
+            b, t = stats(pair, k)
+            dq = jnp.zeros((DH, RB), F32)
+            for half in range(2):
+                for j in range(KB // KT):
+                    rows = pl.ds(j * KT, KT)
+                    pr, ds = weigh(r, half, rows, b, t)
+                    lp[half, rows, k * RB:(k + 1) * RB] = pr
+                    ld[half, rows, k * RB:(k + 1) * RB] = ds
+                    dq += jnp.dot(kt[half, :, rows], ds, preferred_element_type=F32)
+            send_dq(r, dq)
+        q = qb[2 * pair:2 * pair + 2].reshape(2 * RB, DH)
+        do = dob[2 * pair:2 * pair + 2].reshape(2 * RB, DH)
+        for e in reversed(range(KB // KT)):
+            for half in range(2):
+                j = (p >> 1) ^ e
+                rows = pl.ds(pl.multiple_of(j * KT, KT), KT)
+                dk = dka[half, rows, :] + jnp.dot(ld[half, rows, :], q, preferred_element_type=F32)
+                dv = dva[half, rows, :] + jnp.dot(lp[half, rows, :], do, preferred_element_type=F32)
+                dks[pl.ds(half * NB + 2 * j, 2)] = (dk * SCALE).astype(BF16).reshape(2, KP, DH)
+                dvs[pl.ds(half * NB + 2 * j, 2)] = dv.astype(BF16).reshape(2, KP, DH)
+                for step in (2 * e + 1, 2 * e):
+                    if step not in HELD:
+                        ship(half, step)
+
+    def lead(i, carry):
+        forward(2 * i)
+        forward(2 * i + 1)
+        send_stats(i)
+        return carry
+
+    def steady(i, carry):
+        lead(i, carry)
+        return rest(i - LAG, carry)
+
+    def rest(i, carry):
+        settle(sr.at[i], st_recv.at[i])
+        backward(i, 0)
+        backward(i, 1)
+        return carry
+
+    dka[...] = jnp.zeros_like(dka)
+    dva[...] = jnp.zeros_like(dva)
+    settle(kb.at[0], l_sem.at[0])
+    settle(vb.at[0], l_sem.at[1])
+    settle_in(0)
+    state = score(0, 0, fresh())
+    pl.semaphore_wait(barrier, 2 * NB + NG - 2)
+
+    mate = 2 * p + 1 - c
+    remote(k_hbm.at[:, cols(mate)], kb.at[1], kv_send, kv_recv, p, m ^ 1)
+    remote(v_hbm.at[:, cols(mate)], vb.at[1], kv_send, kv_recv, p, m ^ 1)
+    for i in range(1, NB):
+        to = p ^ ORDER[i]
+        remote(q_hbm.at[:, cols(2 * to + c)], qb.at[i], in_send.at[0], in_recv.at[i, 0], to, m)
+        remote(do_hbm.at[:, cols(2 * to + c)], dob.at[i], in_send.at[1], in_recv.at[i, 1], to, m)
+
+    kt[0] = kb[0].T
+    settle(kb, kv_recv)
+    finish(0, score(0, 1, state))
+    forward(1)
+    send_stats(0)
+    kt[1] = kb[1].T
+    lax.fori_loop(1, LAG, lead, 0)
+    lax.fori_loop(LAG, NB // 2, steady, 0)
+    lax.fori_loop(NB // 2 - LAG, NB // 2 - 1, rest, 0)
+    for batch in range(EARLY):
+        finals(batch)
+    settle(sr.at[NB // 2 - 1], st_recv.at[NB // 2 - 1])
+    backward_last()
+    for batch in range(EARLY, NB // BATCH):
+        finals(batch)
+    for step in HELD:
+        for half in (1, 0):
+            ship(half, step)
 
     settle(kb, kv_send)
     settle(qb.at[1:], in_send.at[0])
@@ -269,6 +308,8 @@
             pltpu.VMEM((NB, 2, KB, RB), F32),
             pltpu.VMEM((NB, 8, 128), F32),
             pltpu.VMEM((NB // 2, NG, 2, 8, 128), F32),
+            pltpu.VMEM((2, KB, 2 * RB), BF16),
+            pltpu.VMEM((2, KB, 2 * RB), BF16),
             pltpu.VMEM((2, KB, DH), F32),
             pltpu.VMEM((2, KB, DH), F32),
             pltpu.VMEM((2 * NB, KP, DH), BF16),

time: 61.9 us -> 59.5 us (0.961)
  Pallas kernels: 61.2 us -> 58.6 us
    pallas_call x1, Pallas kernels: 59.1 us -> 56.6 us  [shards(): pl.pallas_call(kernel, out_shape=(jax.ShapeDtypeStruct((8, width), F32),...]
where the time goes in v3:
time: 59.5 us; the launch traced here: 59.4 us
  Pallas kernels  58.6 us (98%)
  between operations  0.8 us (1%)
    pallas_call x1, Pallas kernels, shards(): pl.pallas_call(kernel, out_shape=(jax.ShapeDtypeStruct((8, width), F32),...  56.6 us
    pallas_call x1, Pallas kernels, shards(): pl.pallas_call(place, out_shape=(jax.ShapeDtypeStruct((8, width), F32), j...  2.04 us

profile of v3, /device:TPU:1, one launch (start us, length us, event | category | flops | bytes accessed | tf_op | source)
XLA Modules:
  0.0 59.4 jit_solution(2118854415085714934)
XLA Ops:
  0.6 56.6 %shard_map.67 = (f32[8,2048]{1,0:T(8,128)}, bf16[128,2048]{1,0:T(8,128)(2,1)}, bf16[128,2048]{1,0:T(8,128)(2,1)}) custom-call(bf16[256,2048]{1,0:T(8,128)(2,1)} %q_hbm.1, bf16[1024,2048]{1,0:T(8,128)(2,1)} %k_hbm.1, bf16[1024,2048]{1,0:T(8,128)(2,1)} %v_hbm.1, bf16[256,2048]{1,0:T(8,128)(2,1)} %do_hbm.1), custom_call_target="tpu_custom_call" | custom-call | flops 5368709120 | bytes 12582912 | tf_op jit(solution)/shard_map/pallas_call | solution.py:292
  57.2 2.0 %shard_map.68 = (f32[8,2048]{1,0:T(8,128)}, bf16[1,128,2048]{2,1,0:T(8,128)(2,1)}, bf16[1,128,2048]{2,1,0:T(8,128)(2,1)}) custom-call(f32[8,2048]{1,0:T(8,128)} %get-tuple-element.6.dq, bf16[128,2048]{1,0:T(8,128)(2,1)} %get-tuple-element.7.dk, bf16[128,2048]{1,0:T(8,128)(2,1)} %get-tuple-element.8.dv), custom_call_target="tpu_custom_call" | custom-call | tf_op jit(solution)/shard_map/pallas_call | solution.py:339

commit v4 on v3

--- a/solution.py
+++ b/solution.py
@@ -49,6 +49,12 @@
             src_ref=src, dst_ref=dst, send_sem=send, recv_sem=recv,
             device_id=(pb, mem), device_id_type=MESH,
         ).start()
+
+    def others():
+        for ahead in (4, 3, 5, 2, 6, 1, 7, 0):
+            for flip in (0, NG):
+                if ahead or flip:
+                    yield (m // NG * NG + flip) % (2 * NG) + (m + 2 * ahead) % NG
 
     def settle(ref, sem):
         pltpu.make_async_copy(ref, ref, sem).wait()
@@ -106,8 +112,8 @@
     def send_stats(i):
         pair = pl.ds(2 * i, 2)
         local(st.at[pair], sr.at[i, g], st_recv.at[i])
-        for n in range(1, NG):
-            remote(st.at[pair], sr.at[i, g], st_send, st_recv.at[i], p, m ^ (2 * n))
+        for to in others():
+            remote(st.at[pair], sr.at[i, g], st_send, st_recv.at[i], p, to)
 
     def stats(i, k):
         part = sr[i, :, k]
@@ -138,8 +144,8 @@
         @pl.when(k == BATCH - 1)
         def _():
             local(dqs.at[batch, g], dqr.at[batch, g], dq_recv.at[batch])
-            for i in range(1, NG):
-                remote(dqs.at[batch, g ^ i], dqr.at[batch, g], dq_send, dq_recv.at[batch], p, m ^ (2 * i))
+            for to in others():
+                remote(dqs.at[batch, to // 2], dqr.at[batch, g], dq_send, dq_recv.at[batch], p, to)
 
     def backward(i, k):
         r = 2 * i + k

time: 59.5 us -> 58.8 us (0.988)
  Pallas kernels: 58.6 us -> 57.9 us
    pallas_call x1, Pallas kernels: 56.6 us -> 55.9 us  [shards(): pl.pallas_call(kernel, out_shape=(jax.ShapeDtypeStruct((8, width), F32),...]
where the time goes in v4:
time: 58.8 us; the launch traced here: 58.7 us
  Pallas kernels  57.9 us (98%)
  between operations  0.8 us (1%)
    pallas_call x1, Pallas kernels, shards(): pl.pallas_call(kernel, out_shape=(jax.ShapeDtypeStruct((8, width), F32),...  55.9 us
    pallas_call x1, Pallas kernels, shards(): pl.pallas_call(place, out_shape=(jax.ShapeDtypeStruct((8, width), F32), j...  2.04 us

profile of v4, /device:TPU:1, one launch (start us, length us, event | category | flops | bytes accessed | tf_op | source)
XLA Modules:
  0.0 58.7 jit_solution(18143891019961028365)
XLA Ops:
  0.6 55.9 %shard_map.67 = (f32[8,2048]{1,0:T(8,128)}, bf16[128,2048]{1,0:T(8,128)(2,1)}, bf16[128,2048]{1,0:T(8,128)(2,1)}) custom-call(bf16[256,2048]{1,0:T(8,128)(2,1)} %q_hbm.1, bf16[1024,2048]{1,0:T(8,128)(2,1)} %k_hbm.1, bf16[1024,2048]{1,0:T(8,128)(2,1)} %v_hbm.1, bf16[256,2048]{1,0:T(8,128)(2,1)} %do_hbm.1), custom_call_target="tpu_custom_call" | custom-call | flops 5368709120 | bytes 12582912 | tf_op jit(solution)/shard_map/pallas_call | solution.py:298
  56.5 2.0 %shard_map.68 = (f32[8,2048]{1,0:T(8,128)}, bf16[1,128,2048]{2,1,0:T(8,128)(2,1)}, bf16[1,128,2048]{2,1,0:T(8,128)(2,1)}) custom-call(f32[8,2048]{1,0:T(8,128)} %get-tuple-element.6.dq, bf16[128,2048]{1,0:T(8,128)(2,1)} %get-tuple-element.7.dk, bf16[128,2048]{1,0:T(8,128)(2,1)} %get-tuple-element.8.dv), custom_call_target="tpu_custom_call" | custom-call | tf_op jit(solution)/shard_map/pallas_call | solution.py:345

commit v5 on v4

--- a/solution.py
+++ b/solution.py
@@ -19,7 +19,7 @@
 LAG = 3
 BATCH = 2
 ORDER = (0, 6, 7, 5, 2, 4, 3, 1)
-EARLY = 0
+EARLY = 1
 HELD = (0,)
 SCALE = DH ** -0.5
 C2 = SCALE * math.log2(math.e)

time: 58.8 us -> 60.3 us (1.026)
  Pallas kernels: 57.9 us -> 59.4 us
    pallas_call x1, Pallas kernels: 55.9 us -> 57.3 us  [shards(): pl.pallas_call(kernel, out_shape=(jax.ShapeDtypeStruct((8, width), F32),...]
where the time goes in v5:
time: 60.3 us; the launch traced here: 60.2 us
  Pallas kernels  59.4 us (99%)
  between operations  0.8 us (1%)
    pallas_call x1, Pallas kernels, shards(): pl.pallas_call(kernel, out_shape=(jax.ShapeDtypeStruct((8, width), F32),...  57.3 us
    pallas_call x1, Pallas kernels, shards(): pl.pallas_call(place, out_shape=(jax.ShapeDtypeStruct((8, width), F32), j...  2.04 us

profile of v5, /device:TPU:1, one launch (start us, length us, event | category | flops | bytes accessed | tf_op | source)
XLA Modules:
  0.0 60.2 jit_solution(11259430490006706033)
XLA Ops:
  0.6 57.3 %shard_map.67 = (f32[8,2048]{1,0:T(8,128)}, bf16[128,2048]{1,0:T(8,128)(2,1)}, bf16[128,2048]{1,0:T(8,128)(2,1)}) custom-call(bf16[256,2048]{1,0:T(8,128)(2,1)} %q_hbm.1, bf16[1024,2048]{1,0:T(8,128)(2,1)} %k_hbm.1, bf16[1024,2048]{1,0:T(8,128)(2,1)} %v_hbm.1, bf16[256,2048]{1,0:T(8,128)(2,1)} %do_hbm.1), custom_call_target="tpu_custom_call" | custom-call | flops 5368709120 | bytes 12582912 | tf_op jit(solution)/shard_map/pallas_call | solution.py:298
  58.0 2.0 %shard_map.68 = (f32[8,2048]{1,0:T(8,128)}, bf16[1,128,2048]{2,1,0:T(8,128)(2,1)}, bf16[1,128,2048]{2,1,0:T(8,128)(2,1)}) custom-call(f32[8,2048]{1,0:T(8,128)} %get-tuple-element.6.dq, bf16[128,2048]{1,0:T(8,128)(2,1)} %get-tuple-element.7.dk, bf16[128,2048]{1,0:T(8,128)(2,1)} %get-tuple-element.8.dv), custom_call_target="tpu_custom_call" | custom-call | tf_op jit(solution)/shard_map/pallas_call | solution.py:345
